TPU v7x, 512 devices: a whole 4x8x8 slice. The times are simulated.
512 devices in a mesh: dp: 32 (over y, x), shard: 16 (over z, core).
Axes of the slice: x: 4, y: 8, z: 8, core: 2. Of those that a mesh axis runs over, the one named last changes fastest.
Arguments:
- partials: bfloat16 [32, 128, 256, 256], P('dp', 'shard'), may hold values from -6 to 6
- params: float32 [128, 256, 256], P('shard', 'dp'), may hold values from -0.75 to 0.75
- left_basis: float32 [32, 16, 1, 256, 256], P('dp', 'shard'), may hold values from -0.375 to 0.375
- right_basis: float32 [32, 16, 1, 256, 256], P('dp', 'shard'), may hold values from -0.375 to 0.375
- first_moment: float32 [32, 16, 1, 256, 256], P('dp', 'shard'), may hold values from -4 to 4
- second_moment: float32 [32, 16, 1, 256, 256], P('dp', 'shard'), may hold values from 0.1 to 10
- owner_list: int32 [128], replicated, may hold values from 0 to 511, as said below
Outputs:
- updated: float32 [128, 256, 256], P('shard')
- first_out: float32 [32, 16, 1, 256, 256], P('dp', 'shard')
- second_out: float32 [32, 16, 1, 256, 256], P('dp', 'shard')
Inputs may be any that keep to these rules, and one draw needn't show every extreme that they name: `owner_list`: each owner device is named by at most 1 block, and some device by exactly 1.
All inputs are finite; a program needn't handle non-finite values.
Results may differ from a plain program's by a relative error of at most 0.0003.
Values sent between devices are 32-bit elements; how exact they have to be, the bound alone decides.
A program may use at most 64 MiB of HBM per device.

v0:
```python
import jax
import jax.numpy as jnp
from jax import lax
from jax.sharding import PartitionSpec as P

beta_one = 0.9
beta_two = 0.95
epsilon = 1e-08
learn_rate = 0.2
decay_rate = 0.1
step_count = 10


def local(partials, params, left_basis, right_basis, first_moment, second_moment, owner_list):
    highest = lax.Precision.HIGHEST
    shard_here = lax.axis_index("shard")
    data_here = lax.axis_index("dp")
    shard_count = lax.axis_size("shard")
    data_count = lax.axis_size("dp")
    home_count = params.shape[0]
    row_count = params.shape[1]
    width = params.shape[2]
    slot_count = first_moment.shape[2]
    block_total = owner_list.shape[0]
    summed = lax.psum_scatter(
        partials[0].astype(jnp.float32), "dp", scatter_dimension=1, tiled=True
    )
    home_owner = lax.dynamic_slice_in_dim(owner_list, shard_here * home_count, home_count)
    column_ids = jnp.arange(shard_count, dtype=jnp.int32)
    column_mask = (home_owner[None, :] % shard_count == column_ids[:, None]).astype(jnp.float32)
    outgoing = column_mask[:, :, None, None] * summed[None]
    arrived = lax.all_to_all(outgoing, "shard", split_axis=0, concat_axis=0, tiled=True).reshape(
        block_total, row_count, width
    )
    dest_ids = jnp.arange(data_count, dtype=jnp.int32)
    slot_ids = jnp.arange(slot_count, dtype=jnp.int32)
    owner_match = owner_list[None, None, :] == dest_ids[None, :, None] * shard_count + shard_here
    slot_match = slot_ids[:, None, None] == 0
    picker = (owner_match & slot_match).astype(jnp.float32)
    outgoing_rows = jnp.einsum("kob,brj->korj", picker, arrived, precision=highest)
    whole = lax.all_to_all(outgoing_rows, "dp", split_axis=1, concat_axis=1, tiled=True).reshape(
        slot_count, width, width
    )
    left_mats = left_basis[0, 0]
    right_mats = right_basis[0, 0]
    first_old = first_moment[0, 0]
    second_old = second_moment[0, 0]
    partway = jnp.einsum("cia,cij->caj", left_mats, whole, precision=highest)
    rotated = jnp.einsum("caj,cjb->cab", partway, right_mats, precision=highest)
    first_new = beta_one * first_old + (1.0 - beta_one) * rotated
    second_new = beta_two * second_old + (1.0 - beta_two) * rotated * rotated
    correct_one = 1.0 - beta_one**step_count
    correct_two = 1.0 - beta_two**step_count
    scaled = first_new / correct_one / (jnp.sqrt(second_new / correct_two) + epsilon)
    back_rot = jnp.einsum("cab,cjb->caj", scaled, right_mats, precision=highest)
    change = jnp.einsum("cia,caj->cij", left_mats, back_rot, precision=highest)
    leaving = change.reshape(slot_count, data_count, row_count, width)
    coming = lax.all_to_all(leaving, "dp", split_axis=1, concat_axis=1, tiled=True)
    back_rows = jnp.einsum("kob,korj->brj", picker, coming, precision=highest)
    sending = back_rows.reshape(shard_count, home_count, row_count, width)
    returned = jnp.sum(
        lax.all_to_all(sending, "shard", split_axis=0, concat_axis=0, tiled=True), axis=0
    )
    new_home = params - learn_rate * (returned + decay_rate * params)
    updated = lax.all_gather(new_home, "dp", axis=1, tiled=True)
    my_id = data_here * shard_count + shard_here
    my_count = jnp.sum((owner_list == my_id).astype(jnp.int32))
    live_slot = (slot_ids < my_count)[:, None, None]
    first_keep = jnp.where(live_slot, first_new, first_old)
    second_keep = jnp.where(live_slot, second_new, second_old)
    return (updated, first_keep[None, None], second_keep[None, None])


def solution(mesh):
    return jax.shard_map(
        local,
        mesh=mesh,
        in_specs=(
            P("dp", "shard", None, None),
            P("shard", "dp", None),
            P("dp", "shard", None, None, None),
            P("dp", "shard", None, None, None),
            P("dp", "shard", None, None, None),
            P("dp", "shard", None, None, None),
            P(),
        ),
        out_specs=(
            P("shard", None, None),
            P("dp", "shard", None, None, None),
            P("dp", "shard", None, None, None),
        ),
        check_vma=False,
    )
```

profile of v0, /device:TPU:8, one launch (start us, length us, event | category | flops | bytes accessed | tf_op | source)
XLA Modules:
  0.0 433.2 jit_solution(3152001172057728379)
XLA Ops:
  7.2 0.0 copy-start
  7.2 0.0 copy-start.5
  7.2 0.0 reduce-scatter.2.cloned.1.call-start
  7.2 2.8 bitcast_convert_fusion
  10.0 0.0 reduce-scatter.2.cloned.1.call-update
  10.0 0.0 copy-done.5
  10.0 0.1 and_select_fusion
  10.1 227.9 %reduce-scatter.2.cloned.1.call-done = f32[8,8,256]{2,1,0:T(8,128)} async-done(((f32[8,256,256]{2,1,0:T(8,128)}), f32[8,8,256]{2,1,0:T(8,128)}) %reduce-scatter.2.cloned.1.call-update) | async-done | bytes 65552 | tf_op jit(solution)/shard_map/reduce_scatter | solution.py:25
  238.0 0.9 copy.24
  238.9 1.1 broadcast_multiply_fusion
  240.0 7.4 %all-to-all-start = ((f32[16,8,8,256]{3,1,2,0:T(8,128)}), f32[16,8,8,256]{3,1,2,0:T(8,128)S(1)}, u32[]{:S(2)}, u32[]{:S(2)}) async-start(f32[16,8,8,256]{3,1,2,0:T(8,128)} %broadcast_multiply_fusion), calls=%async_computation.1 | async-start | bytes 2097152 | tf_op jit(solution)/shard_map/all_to_all | solution.py:32
  247.5 0.0 copy-start.1
  247.5 0.0 copy-start.2
  247.5 0.0 copy-start.3
  247.5 26.6 %all-to-all-done = f32[16,8,8,256]{3,1,2,0:T(8,128)S(1)} async-done(((f32[16,8,8,256]{3,1,2,0:T(8,128)}), f32[16,8,8,256]{3,1,2,0:T(8,128)S(1)}, u32[]{:S(2)}, u32[]{:S(2)}) %all-to-all-start) | async-done | bytes 1048608 | tf_op jit(solution)/shard_map/all_to_all | solution.py:32
  274.1 0.5 convolution_bitcast_fusion.2
  274.6 0.2 copy.26
  274.8 20.4 %all_to_all.20 = f32[1,32,8,256]{3,2,0,1:T(8,128)S(1)} all-to-all(f32[1,32,8,256]{3,2,0,1:T(8,128)S(1)} %copy.26), channel_id=1, replica_groups=mesh['dp'=32,'shard'=16] {'dp'}, dimensions={1} | all-to-all | bytes 524288 | tf_op jit(solution)/shard_map/all_to_all | solution.py:41
  295.2 0.0 copy-done
  295.2 0.6 fusion.9
  295.8 0.0 copy-done.1
  295.8 0.6 fusion.7
  296.4 0.0 copy-done.2
  296.4 0.0 copy-done.3
  296.4 0.6 convolution_bitcast_fusion.1
  297.0 0.4 convolution_bitcast_fusion
  297.4 0.9 copy.28
  298.3 5.3 %all-to-all-start.2 = ((f32[1,32,8,256]{3,2,0,1:T(8,128)}), f32[1,32,8,256]{3,2,0,1:T(8,128)S(1)}, u32[]{:S(2)}, u32[]{:S(2)}) async-start(f32[1,32,8,256]{3,2,0,1:T(8,128)} %copy.28), calls=%async_computation.3 | async-start | bytes 524288 | tf_op jit(solution)/shard_map/all_to_all | solution.py:58
  303.6 0.0 all-gather.2.cloned.1.call-start
  303.7 0.1 eq.57
  303.8 0.0 copy-start.4
  303.8 12.7 %all-to-all-done.2 = f32[1,32,8,256]{3,2,0,1:T(8,128)S(1)} async-done(((f32[1,32,8,256]{3,2,0,1:T(8,128)}), f32[1,32,8,256]{3,2,0,1:T(8,128)S(1)}, u32[]{:S(2)}, u32[]{:S(2)}) %all-to-all-start.2) | async-done | bytes 262176 | tf_op jit(solution)/shard_map/all_to_all | solution.py:58
  316.5 0.6 fusion.3
  317.1 29.8 %all_to_all.21 = f32[16,8,8,256]{3,1,2,0:T(8,128)S(1)} all-to-all(f32[16,8,8,256]{3,1,2,0:T(8,128)S(1)} %fusion.3), channel_id=1, replica_groups=mesh['dp'=32,'shard'=16] {'shard'}, dimensions={0} | all-to-all | bytes 2097152 | tf_op jit(solution)/shard_map/all_to_all | solution.py:62
  346.9 0.1 reduce_sum.18
  346.9 0.0 copy-done.4
  346.9 0.7 multiply_subtract_fusion
  347.6 0.0 all-gather.2.cloned.1.call-update
  347.6 0.6 fusion.39
  348.9 0.9 fusion.5
  349.8 73.0 %all-gather.2.cloned.1.call-done = f32[8,256,256]{2,0,1:T(8,128)} async-done(((f32[8,8,256]{2,0,1:T(8,128)}), f32[8,256,256]{2,0,1:T(8,128)}) %all-gather.2.cloned.1.call-update) | async-done | bytes 2097168 | tf_op jit(solution)/shard_map/all_gather | solution.py:65
  422.8 3.6 copy.32
  (2 shorter events, 0.0 us)
Async XLA Ops:
  7.2 288.0 %copy-start = (f32[1,1,1,256,256]{4,3,2,1,0:T(8,128)S(1)}, f32[1,1,1,256,256]{4,3,2,1,0:T(8,128)}, u32[]{:S(2)}) copy-start(f32[1,1,1,256,256]{4,3,2,1,0:T(8,128)} %param.9) | copy-start | bytes 786436
  7.2 2.9 copy-start.5
  7.2 230.8 %reduce-scatter.2.cloned.1.call-start = ((), (), s32[]{:S(2)}) async-start(), calls=%async_computation.5 | async-start | bytes 2162688 | tf_op jit(solution)/shard_map/reduce_scatter | solution.py:25
  240.0 34.1 %all-to-all-start = ((f32[16,8,8,256]{3,1,2,0:T(8,128)}), f32[16,8,8,256]{3,1,2,0:T(8,128)S(1)}, u32[]{:S(2)}, u32[]{:S(2)}) async-start(f32[16,8,8,256]{3,1,2,0:T(8,128)} %broadcast_multiply_fusion), calls=%async_computation.1 | async-start | bytes 2097152 | tf_op jit(solution)/shard_map/all_to_all | solution.py:32
  247.5 48.3 %copy-start.1 = (f32[1,1,1,256,256]{4,3,2,1,0:T(8,128)S(1)}, f32[1,1,1,256,256]{4,3,2,1,0:T(8,128)}, u32[]{:S(2)}) copy-start(f32[1,1,1,256,256]{4,3,2,1,0:T(8,128)} %param.10) | copy-start | bytes 786436
  247.5 48.9 %copy-start.2 = (f32[1,1,1,256,256]{4,3,2,1,0:T(8,128)S(1)}, f32[1,1,1,256,256]{4,3,2,1,0:T(8,128)}, u32[]{:S(2)}) copy-start(f32[1,1,1,256,256]{4,3,2,1,0:T(8,128)} %param.11) | copy-start | bytes 786436
  247.5 48.9 %copy-start.3 = (f32[1,1,1,256,256]{4,3,2,1,0:T(8,128)S(1)}, f32[1,1,1,256,256]{4,3,2,1,0:T(8,128)}, u32[]{:S(2)}) copy-start(f32[1,1,1,256,256]{4,3,2,1,0:T(8,128)} %param.12) | copy-start | bytes 786436
  298.3 18.2 %all-to-all-start.2 = ((f32[1,32,8,256]{3,2,0,1:T(8,128)}), f32[1,32,8,256]{3,2,0,1:T(8,128)S(1)}, u32[]{:S(2)}, u32[]{:S(2)}) async-start(f32[1,32,8,256]{3,2,0,1:T(8,128)} %copy.28), calls=%async_computation.3 | async-start | bytes 524288 | tf_op jit(solution)/shard_map/all_to_all | solution.py:58
  303.6 119.2 %all-gather.2.cloned.1.call-start = ((), (), s32[]{:S(2)}) async-start(), calls=%async_computation.6 | async-start | bytes 2162688 | tf_op jit(solution)/shard_map/all_gather | solution.py:65
  303.8 43.2 %copy-start.4 = (f32[8,8,256]{2,1,0:T(8,128)S(1)}, f32[8,8,256]{2,1,0:T(8,128)}, u32[]{:S(2)}) copy-start(f32[8,8,256]{2,1,0:T(8,128)} %param.8) | copy-start | bytes 196612
Sparse Core Ops, SparseCore 0:
  13.0 224.9 reduce-scatter.1
  347.8 75.0 all-gather.1
where the time goes:
time: 434 us; the launch traced here: 433 us
  waiting for transfers between devices  340 us (78%)
  blocking collectives  50.2 us (12%)
  between operations  14.9 us (3%)
  starting transfers between devices  12.9 us (3%)
  other arithmetic  6.2 us (1%)
  local copies, waits for them, and re-layouts  5.58 us (1%)
    reduce_scatter x1, waiting for transfers between devices, local(): lax.psum_scatter(partials[0].astype(jnp.float32), 'dp', scatter_dimension...  228 us
    all_gather x1, waiting for transfers between devices, local(): updated = lax.all_gather(new_home, 'dp', axis=1, tiled=True)  73 us
    all_to_all x1, blocking collectives, local(): lax.all_to_all(sending, 'shard', split_axis=0, concat_axis=0, tiled=True)  29.8 us
    all_to_all x1, waiting for transfers between devices, local(): lax.all_to_all(outgoing, 'shard', split_axis=0, concat_axis=0, tiled=True)  26.6 us
    all_to_all x1, blocking collectives, local(): lax.all_to_all(outgoing_rows, 'dp', split_axis=1, concat_axis=1, tiled=True)  20.4 us
    all_to_all x1, waiting for transfers between devices, local(): lax.all_to_all(leaving, 'dp', split_axis=1, concat_axis=1, tiled=True)  12.7 us
  transfers between devices with their start and end apart: 4, of which 4 were waited for; matrix products, arithmetic and copies ran while one was open for 0% of the time, Pallas kernels for 0%

commit v1 on v0

v1 whole, which is shorter than its diff:
```python
import functools

import jax
import jax.numpy as jnp
from jax import lax
from jax.experimental import pallas as pl
from jax.experimental.pallas import tpu as pltpu
from jax.sharding import PartitionSpec as P

beta_one = 0.9
beta_two = 0.95
epsilon = 1e-08
learn_rate = 0.2
decay_rate = 0.1
step_count = 10

MESH = pl.DeviceIdType.MESH
F32 = jnp.float32
BF16 = jnp.bfloat16
NX, NY, NZ, NC = 4, 8, 8, 2
ND, NS = NX * NY, NZ * NC
HALVES = (0, 1)


def split(value):
    high = value.astype(BF16)
    return high, (value - high.astype(F32)).astype(BF16)


def dot(left, right):
    return jnp.dot(left, right, preferred_element_type=F32)


def dot3(left, right):
    return dot(left[0], right[0]) + (dot(left[0], right[1]) + dot(left[1], right[0]))


def body(
    own_hbm, part_hbm, params_hbm, left_hbm, right_hbm, first_hbm, second_hbm,
    out_hbm, first_out_hbm, second_out_hbm,
    own_vec, own_ref, idx_vec, idx_ref, part, params, left, right, first, second, first_new, second_new,
    acc_x, acc_y, in_x, in_y, small_x, small_y,
    every_0, every_1, chosen, whole, change, coming_0, coming_1, sib_out, sib_in, mine, z_in, fresh,
    l_hi, l_lo, lt_hi, lt_lo, r_hi, r_lo, rt_hi, rt_lo,
    meter, load_sem, idx_sem, send_sem, x_sem, y_sem, sx_sem, sy_sem, z_sem, zs_sem, c_sem, e_sem, fs_sem, f_sem,
    gsy_sem, gsx_sem, gx_sem, gy_sem, keep_sem, out_sem,
):
    d = lax.axis_index("dp")
    s = lax.axis_index("shard")
    y, x = lax.div(d, NX), lax.rem(d, NX)
    z, c = lax.div(s, NC), lax.rem(s, NC)
    f = 1 - 2 * c

    def xs(k):
        return lax.rem(x + k + 2 * NX, NX)

    def ys(k):
        return lax.rem(y + k + 2 * NY, NY)

    def zs(k):
        return lax.rem(z + k + NZ, NZ)

    def at_x(k):
        return (y * NX + xs(k), s)

    def at_y(k):
        return (ys(k) * NX + x, s)

    def at_z(k):
        return (d, zs(k) * NC + c)

    def at_d(k):
        return lax.rem(d + k, ND)

    sibling = (d, z * NC + 1 - c)
    every = (every_0, every_1)
    coming = (coming_0, coming_1)
    sent = [0]
    stores = []

    def send(src, dst, recv, device, tiles):
        copy = pltpu.make_async_remote_copy(
            src_ref=src, dst_ref=dst, send_sem=send_sem.at[0], recv_sem=recv, device_id=device, device_id_type=MESH
        )
        copy.start()
        sent[0] += tiles

    def arrived(ref, sem):
        pltpu.make_async_copy(ref, ref, sem).wait()

    def block_at(slot_index):
        return jnp.maximum(idx_ref[slot_index, 0] - 1, 0)

    def finish():
        arrived(meter.at[pl.ds(0, sent[0])], send_sem.at[0])
        for store in stores:
            store.wait()

    def out_x(h, xi, yi):
        return out_hbm.at[pl.ds(0, 4), yi, xi, :, pl.ds(128 * h, 128)]

    def out_y(h, yi, xi):
        return out_hbm.at[pl.ds(4, 4), yi, xi, :, pl.ds(128 * h, 128)]

    def all_x(h, xi):
        return out_hbm.at[pl.ds(0, 4), :, xi, :, pl.ds(128 * h, 128)]

    def all_y(h, yi):
        return out_hbm.at[pl.ds(4, 4), yi, :, :, pl.ds(128 * h, 128)]

    def in_order(*streams):
        waiting = [(0.0, place, stream) for place, stream in enumerate(streams)]
        while waiting:
            waiting.sort(key=lambda entry: entry[:2])
            _, place, stream = waiting.pop(0)
            time = next(stream, None)
            if time is not None:
                waiting.append((time, place, stream))

    loads = [
        pltpu.make_async_copy(src, dst, load_sem.at[i])
        for i, (src, dst) in enumerate(
            (
                (own_hbm, own_vec), (part_hbm.at[pl.ds(4, 4)], part.at[pl.ds(4, 4)]),
                (part_hbm.at[pl.ds(0, 4)], part.at[pl.ds(0, 4)]),
                (left_hbm, left), (right_hbm, right), (first_hbm, first), (second_hbm, second), (params_hbm, params), (own_hbm, own_ref),
            )
        )
    ]
    for load in loads:
        load.start()

    barrier = pltpu.get_barrier_semaphore()
    for k in range(1, ND):
        pl.semaphore_signal(barrier, inc=1, device_id=(at_d(k), s), device_id_type=MESH)
    for k in range(1, NZ):
        pl.semaphore_signal(barrier, inc=1, device_id=at_z(k), device_id_type=MESH)
    pl.semaphore_signal(barrier, inc=1, device_id=sibling, device_id_type=MESH)

    loads[0].wait()
    block = lax.broadcasted_iota(jnp.int32, (ND, 128), 1)
    home, inner = lax.div(block, 8), lax.rem(block, 8)
    place = ((lax.div(inner, 4) * NC + lax.rem(home, NC)) * NZ + lax.div(home, NC)) * 4 + lax.rem(inner, 4) + 1
    slot = lax.broadcasted_iota(jnp.int32, (ND, 128), 0) * NS + s
    found = jnp.max(jnp.where(own_vec[...] == slot, place, 0), axis=1, keepdims=True)
    idx_vec[...] = jnp.broadcast_to(found, (ND, 128))
    idx_copy = pltpu.make_async_copy(idx_vec, idx_ref, idx_sem.at[0])
    idx_copy.start()

    loads[1].wait()

    @pl.loop(0, 4)
    def _(blk):
        for yi in range(NY):
            rows = part[4 + blk, 32 * yi : 32 * yi + 32, :].astype(F32)
            for xi in range(NX):
                for h in HALVES:
                    acc_y[h, yi, blk, xi] = rows[8 * xi : 8 * xi + 8, 128 * h : 128 * h + 128]

    loads[2].wait()

    @pl.loop(0, 4)
    def _(blk):
        for yi in range(NY):
            rows = part[blk, 32 * yi : 32 * yi + 32, :].astype(F32)
            for xi in range(NX):
                for h in HALVES:
                    acc_x[h, xi, blk, yi] = rows[8 * xi : 8 * xi + 8, 128 * h : 128 * h + 128]

    pl.semaphore_wait(barrier, ND - 1 + NZ - 1 + 1)

    def spread(kind, h, total):
        own = every[h].at[kind, c, z]
        every[h][kind, c, z] = total
        for k in range(1, NZ):
            send(own, own, z_sem.at[h, kind, k - 1], at_z(k), 4)
        send(own, own, zs_sem.at[h, kind], sibling, 4)

    def relay(kind, h):
        for k in (1, 7, 2, 6, 3, 5, 4):
            chunk = every[h].at[kind, c, zs(-k)]
            arrived(chunk, z_sem.at[h, kind, k - 1])
            send(chunk, chunk, zs_sem.at[h, kind], sibling, 4)

    def x_unit(h):
        send(acc_x.at[h, xs(2)], in_x.at[h, 0], x_sem.at[h, 0], at_x(f), 32)
        send(acc_x.at[h, xs(-f)], in_x.at[h, 2], x_sem.at[h, 2], at_x(-f), 32)
        yield 4.4 + 2.5 * h
        arrived(in_x.at[h, 0], x_sem.at[h, 0])
        acc_x[h, xs(f)] += in_x[h, 0]
        send(acc_x.at[h, xs(f)], in_x.at[h, 1], x_sem.at[h, 1], at_x(f), 32)
        yield 8.2 + 1.3 * h
        arrived(in_x.at[h, 2], x_sem.at[h, 2])
        arrived(in_x.at[h, 1], x_sem.at[h, 1])
        acc_x[h, x] += in_x[h, 1] + in_x[h, 2]
        for k in range(1, NY):
            send(acc_x.at[h, x, :, ys(k)], small_y.at[h, k - 1], sy_sem.at[h], at_y(k), 4)
        yield 12.5 + 2.0 * h
        arrived(small_y.at[h], sy_sem.at[h])
        total = acc_x[h, x, :, y]
        for k in range(NY - 1):
            total += small_y[h, k]
        spread(0, h, total)
        yield 17.0 + 3.0 * h
        relay(0, h)

    def y_unit(h):
        send(acc_y.at[h, ys(4)], in_y.at[h, 0], y_sem.at[h, 0], at_y(f), 16)
        send(acc_y.at[h, ys(-3 * f)], in_y.at[h, 4], y_sem.at[h, 4], at_y(-f), 16)
        for step in range(3):
            yield 3.0 * (step + 1) + 1.3 * h
            arrived(in_y.at[h, step], y_sem.at[h, step])
            far = ys((3 - step) * f)
            acc_y[h, far] += in_y[h, step]
            send(acc_y.at[h, far], in_y.at[h, step + 1], y_sem.at[h, step + 1], at_y(f), 16)
            if step < 2:
                arrived(in_y.at[h, 4 + step], y_sem.at[h, 4 + step])
                far = ys(-(2 - step) * f)
                acc_y[h, far] += in_y[h, 4 + step]
                send(acc_y.at[h, far], in_y.at[h, 5 + step], y_sem.at[h, 5 + step], at_y(-f), 16)
        yield 12.0 + 1.3 * h
        arrived(in_y.at[h, 3], y_sem.at[h, 3])
        arrived(in_y.at[h, 6], y_sem.at[h, 6])
        acc_y[h, y] += in_y[h, 3] + in_y[h, 6]
        for k in range(1, NX):
            send(acc_y.at[h, y, :, xs(k)], small_x.at[h, k - 1], sx_sem.at[h], at_x(k), 4)
        yield 14.5 + 1.3 * h
        arrived(small_x.at[h], sx_sem.at[h])
        total = acc_y[h, y, :, x]
        for k in range(NX - 1):
            total += small_x[h, k]
        spread(1, h, total)
        yield 19.0 + 3.0 * h
        relay(1, h)

    def bases():
        yield 2.0
        for load in loads[3:]:
            load.wait()
        idx_copy.wait()
        value = left[...]
        l_hi[...], l_lo[...] = split(value)
        yield 2.1
        lt_hi[...], lt_lo[...] = split(left[...].T)
        yield 5.0
        value = right[...]
        r_hi[...], r_lo[...] = split(value)
        yield 8.0
        rt_hi[...], rt_lo[...] = split(right[...].T)

    def to_owners(h):
        yield 21.0 + 3.0 * h
        for kind in range(2):
            arrived(every[h].at[kind, 1 - c], zs_sem.at[h, kind])
        flat = every[h].reshape(128, 8, 128)
        whole[h, d] = flat[block_at(d)]
        for k in range(1, ND):
            to = at_d(k)
            chosen[h, to] = flat[block_at(to)]
            send(chosen.at[h, to], whole.at[h, d], c_sem.at[h], (to, s), 1)

    in_order(y_unit(0), x_unit(0), y_unit(1), x_unit(1), bases(), to_owners(0), to_owners(1))

    partway = []
    for h in HALVES:
        arrived(whole.at[h, pl.ds(0, ND - 1)], c_sem.at[h])
        partway.append(dot3((lt_hi[...], lt_lo[...]), split(whole[h].reshape(256, 128))))
    rotated = dot3(split(partway[0]), (r_hi[0:128], r_lo[0:128])) + dot3(
        split(partway[1]), (r_hi[128:256], r_lo[128:256])
    )
    first_old, second_old = first[...], second[...]
    first_val = beta_one * first_old + (1.0 - beta_one) * rotated
    second_val = beta_two * second_old + (1.0 - beta_two) * rotated * rotated
    correct_one = 1.0 - beta_one**step_count
    correct_two = 1.0 - beta_two**step_count
    scaled = split(first_val / correct_one / (jnp.sqrt(second_val / correct_two) + epsilon))
    for h in HALVES:
        back = dot3(scaled, (rt_hi[:, 128 * h : 128 * h + 128], rt_lo[:, 128 * h : 128 * h + 128]))
        change[h] = dot3((l_hi[...], l_lo[...]), split(back)).reshape(ND, 8, 128)
        coming[h][d] = change[h, d]
        for k in range(1, ND):
            to = at_d(k)
            send(change.at[h, to], coming[h].at[d], e_sem.at[h], (to, s), 1)
    live = idx_ref[d, 0] > 0
    first_new[...] = jnp.where(live, first_val, first_old)
    second_new[...] = jnp.where(live, second_val, second_old)
    stores.append(pltpu.make_async_copy(first_new, first_out_hbm, out_sem.at[0]))
    stores.append(pltpu.make_async_copy(second_new, second_out_hbm, out_sem.at[1]))
    for store in stores:
        store.start()

    def rows_of(kind, h, zi, core, blk):
        who = own_ref[0, (zi * NC + core) * 8 + 4 * kind + blk]
        return jnp.where((who & (NS - 1)) == s, coming[h][who >> 4], 0.0)

    def gather_sibling(kind, h):
        for zi in range(NZ):
            for blk in range(4):
                sib_out[h, kind, zi, blk] = rows_of(kind, h, zi, 1 - c, blk)
        send(sib_out.at[h, kind], sib_in.at[h, kind], fs_sem.at[h, kind], sibling, 32)

    def gather_mine(kind, h):
        for zi in range(NZ):
            for blk in range(4):
                mine[h, kind, zi, blk] = rows_of(kind, h, zi, c, blk)

    def home_sends(kind, h):
        arrived(sib_in.at[h, kind], fs_sem.at[h, kind])
        for k in range(1, NZ):
            mine[h, kind, zs(k)] += sib_in[h, kind, zs(k)]
            send(mine.at[h, kind, zs(k)], z_in.at[h, kind, k - 1], f_sem.at[h, kind], at_z(k), 4)

    def home_rows(kind, h):
        arrived(z_in.at[h, kind], f_sem.at[h, kind])
        total = mine[h, kind, z] + sib_in[h, kind, z]
        for k in range(NZ - 1):
            total += z_in[h, kind, k]
        old = params[4 * kind : 4 * kind + 4, :, 128 * h : 128 * h + 128]
        fresh[h, kind] = old - learn_rate * (total + decay_rate * old)

    def y_back(h):
        yield 0.0 + 2.0 * h
        arrived(coming[h].at[pl.ds(0, ND - 1)], e_sem.at[h])
        gather_sibling(1, h)
        gather_sibling(0, h)
        gather_mine(1, h)
        yield 1.5 + 2.0 * h
        home_sends(1, h)
        yield 6.5 + 2.0 * h
        home_rows(1, h)
        pltpu.make_async_copy(fresh.at[h, 1], out_y(h, y, x), keep_sem.at[h, 1]).start()
        for k in range(1, NX):
            send(fresh.at[h, 1], out_y(h, y, x), gsx_sem.at[h], at_x(k), 4)
        yield 9.0 + 2.0 * h
        arrived(fresh.at[h, 1], keep_sem.at[h, 1])
        arrived(all_y(h, 0).at[:, pl.ds(0, NX - 1)], gsx_sem.at[h])
        send(all_y(h, y), all_y(h, y), gy_sem.at[h, 0], at_y(f), 16)
        send(all_y(h, y), all_y(h, y), gy_sem.at[h, 4], at_y(-f), 16)
        for step in range(4):
            yield 12.0 + 3.0 * step + 1.5 * h
            chunk = all_y(h, ys(-(step + 1) * f))
            arrived(chunk, gy_sem.at[h, step])
            if step < 3:
                send(chunk, chunk, gy_sem.at[h, step + 1], at_y(f), 16)
                chunk = all_y(h, ys((step + 1) * f))
                arrived(chunk, gy_sem.at[h, 4 + step])
                if step < 2:
                    send(chunk, chunk, gy_sem.at[h, 5 + step], at_y(-f), 16)

    def x_back(h):
        yield 4.0 + 1.0 * h
        gather_mine(0, h)
        home_sends(0, h)
        yield 10.0 + 2.0 * h
        home_rows(0, h)
        pltpu.make_async_copy(fresh.at[h, 0], out_x(h, x, y), keep_sem.at[h, 0]).start()
        for k in range(1, NY):
            send(fresh.at[h, 0], out_x(h, x, y), gsy_sem.at[h], at_y(k), 4)
        yield 14.0 + 2.0 * h
        arrived(fresh.at[h, 0], keep_sem.at[h, 0])
        arrived(all_x(h, 0).at[:, pl.ds(0, NY - 1)], gsy_sem.at[h])
        send(all_x(h, x), all_x(h, x), gx_sem.at[h, 0], at_x(f), 32)
        send(all_x(h, x), all_x(h, x), gx_sem.at[h, 2], at_x(-f), 32)
        yield 18.0 + 2.5 * h
        chunk = all_x(h, xs(-f))
        arrived(chunk, gx_sem.at[h, 0])
        send(chunk, chunk, gx_sem.at[h, 1], at_x(f), 32)
        yield 23.0 + 2.5 * h
        arrived(all_x(h, xs(f)), gx_sem.at[h, 2])
        arrived(all_x(h, xs(2)), gx_sem.at[h, 1])

    in_order(y_back(0), y_back(1), x_back(0), x_back(1))
    finish()


def local(partials, params, left_basis, right_basis, first_moment, second_moment, owner_list):
    dma = pltpu.SemaphoreType.DMA
    full = (256, 256)
    vm = pltpu.VMEM
    any_spec = pl.BlockSpec(memory_space=pl.ANY)
    in_hbm = functools.partial(pltpu.with_memory_space_constraint, memory_space=pltpu.HBM)
    updated, first_out, second_out = pl.pallas_call(
        body,
        out_shape=(
            pltpu.VMEM((8, NY, NX, 8, 256), F32),
            pltpu.VMEM(full, F32),
            pltpu.VMEM(full, F32),
        ),
        in_specs=[any_spec] * 7,
        out_specs=(any_spec,) * 3,
        scratch_shapes=[
            vm((1, 128), jnp.int32), pltpu.SMEM((1, 128), jnp.int32), vm((ND, 128), jnp.int32), pltpu.SMEM((ND, 128), jnp.int32),
            vm((8, 256, 256), BF16), vm((8, 8, 256), F32),
            vm(full, F32), vm(full, F32), vm(full, F32), vm(full, F32), vm(full, F32), vm(full, F32),
            vm((2, NX, 4, NY, 8, 128), F32), vm((2, NY, 4, NX, 8, 128), F32),
            vm((2, 3, 4, NY, 8, 128), F32), vm((2, 7, 4, NX, 8, 128), F32),
            vm((2, NX - 1, 4, 8, 128), F32), vm((2, NY - 1, 4, 8, 128), F32),
            vm((2, NC, NZ, 4, 8, 128), F32), vm((2, NC, NZ, 4, 8, 128), F32),
            vm((2, ND, 8, 128), F32), vm((2, ND, 8, 128), F32),
            vm((2, ND, 8, 128), F32), vm((ND, 8, 128), F32), vm((ND, 8, 128), F32),
            vm((2, 2, NZ, 4, 8, 128), F32), vm((2, 2, NZ, 4, 8, 128), F32), vm((2, 2, NZ, 4, 8, 128), F32),
            vm((2, 2, NZ - 1, 4, 8, 128), F32), vm((2, 2, 4, 8, 128), F32),
            vm(full, BF16), vm(full, BF16), vm(full, BF16), vm(full, BF16),
            vm(full, BF16), vm(full, BF16), vm(full, BF16), vm(full, BF16),
            vm((3072, 8, 128), F32),
            dma((9,)), dma((1,)), dma((1,)), dma((2, 3)), dma((2, 7)), dma((2,)), dma((2,)), dma((2, 2, 7)), dma((2, 2)),
            dma((2,)), dma((2,)), dma((2, 2)), dma((2, 2)), dma((2,)), dma((2,)), dma((2, 3)), dma((2, 7)), dma((2, 2)),
            dma((2,)),
        ],
        compiler_params=pltpu.CompilerParams(
            collective_id=0, has_side_effects=True, vmem_limit_bytes=48 * 1024 * 1024
        ),
        name="soap_step",
    )(
        *map(
            in_hbm,
            (
                owner_list.reshape(1, 128), partials[0], params, left_basis[0, 0, 0], right_basis[0, 0, 0],
                first_moment[0, 0, 0], second_moment[0, 0, 0],
            ),
        )
    )
    return (
        updated.reshape(8, 256, 256),
        first_out[None, None, None],
        second_out[None, None, None],
    )


def solution(mesh):
    return jax.shard_map(
        local,
        mesh=mesh,
        in_specs=(
            P("dp", "shard", None, None),
            P("shard", "dp", None),
            P("dp", "shard", None, None, None),
            P("dp", "shard", None, None, None),
            P("dp", "shard", None, None, None),
            P("dp", "shard", None, None, None),
            P(),
        ),
        out_specs=(
            P("shard", None, None),
            P("dp", "shard", None, None, None),
            P("dp", "shard", None, None, None),
        ),
        check_vma=False,
    )
```

time: 434 us -> 101 us (0.23)
  waiting for transfers between devices: 340 us -> 0 us
  Pallas kernels: 0 us -> 98 us
  blocking collectives: 50.2 us -> 0 us
  between operations: 14.9 us -> 0.64 us
  starting transfers between devices: 12.9 us -> 0 us
  other arithmetic: 6.2 us -> 0 us
    reduce_scatter x1 -> x0, waiting for transfers between devices: 228 us -> none  [local(): lax.psum_scatter(partials[0].astype(jnp.float32), 'dp', scatter_dimension...]
    pallas_call x0 -> x1, Pallas kernels: none -> 98 us  [local(): pl.pallas_call(body, out_shape=(pltpu.VMEM((8, NY, NX, 8, 256), F32), plt...]
    all_gather x1 -> x0, waiting for transfers between devices: 73 us -> none  [local(): updated = lax.all_gather(new_home, 'dp', axis=1, tiled=True)]
    all_to_all x2 -> x0, blocking collectives: 50.2 us -> none  [the longest x1 29.8 us: local(): lax.all_to_all(sending, 'shard', split_axis=0, concat_axis=0, tiled=True)]
    all_to_all x2 -> x0, waiting for transfers between devices: 39.3 us -> none  [the longest x1 26.6 us: local(): lax.all_to_all(outgoing, 'shard', split_axis=0, concat_axis=0, tiled=True)]
    all_to_all x2 -> x0, starting transfers between devices: 12.8 us -> none  [the longest x1 7.44 us: local(): lax.all_to_all(outgoing, 'shard', split_axis=0, concat_axis=0, tiled=True)]
  transfers between devices with their start and end apart: 4 -> 0, of which waited for: 4 -> 0; matrix products, arithmetic and copies ran while one was open for 0% -> 0% of each run, Pallas kernels for 0% -> 0%
where the time goes in v1:
time: 101 us
  Pallas kernels  98 us (97%)
  local copies, waits for them, and re-layouts  2.73 us (3%)
    pallas_call x1, Pallas kernels, local(): pl.pallas_call(body, out_shape=(pltpu.VMEM((8, NY, NX, 8, 256), F32), plt...  98 us
    unnamed x3, local copies, waits for them, and re-layouts  2.73 us

profile of v1, /device:TPU:8, one launch (start us, length us, event | category | flops | bytes accessed | tf_op | source)
XLA Modules:
  0.0 101.3 jit_solution(15528259323260369952)
XLA Ops:
  0.6 98.0 %soap_step.1 = (f32[8,8,4,8,256]{4,3,2,1,0:T(8,128)S(1)}, f32[256,256]{1,0:T(8,128)S(1)}, f32[256,256]{1,0:T(8,128)S(1)}) custom-call(s32[1,128]{1,0:T(1,128)} %bitcast.17, bf16[8,256,256]{2,1,0:T(8,128)(2,1)} %bitcast.12, f32[8,8,256]{2,1,0:T(8,128)} %params_hbm.1, f32[256,256]{1,0:T(8,128)} %bitcast.13, f32[256,256]{1,0:T(8,128)} %bitcast.14, ...), custom_call_target="tpu_custom_call" | custom-call | tf_op jit(solution)/shard_map/soap_step/pallas_call | solution.py:382
  98.6 1.3 %copy.13 = f32[8,256,256]{2,1,0:T(8,128)} copy(f32[8,256,256]{2,1,0:T(8,128)S(1)} %bitcast.9) | data formatting | bytes 4194304
  99.9 0.7 copy.14
  100.6 0.7 copy.15

commit v2 on v1

--- a/solution.py
+++ b/solution.py
@@ -21,6 +21,43 @@
 ND, NS = NX * NY, NZ * NC
 HALVES = (0, 1)
 
+TIMES = {
+    "x0": (5, 3),
+    "x1": (9, 3),
+    "x2": (14, 3),
+    "x3": (17.1, 3.0),
+    "x4": (20.6, 3.0),
+    "y0": (3, 1.5),
+    "y1": (6, 1.5),
+    "y2": (9, 1.5),
+    "y3": (12, 2),
+    "y4": (14.2, 2.2),
+    "y5": (17, 3.0),
+    "y6": (20.5, 3.0),
+    "c": (20.7, 3.0),
+    "b0": (0, 2),
+    "b00": (1.5, 2),
+    "b1": (1.6, 2),
+    "b2": (4.5, 2),
+    "b3": (7.5, 2),
+    "b4": (10.5, 2),
+    "g0": (14.5, 1.5),
+    "g1": (17.5, 1.5),
+    "g2": (20.5, 1.5),
+    "g3": (23.5, 1.5),
+    "a0": (2.0, 2),
+    "a1": (5.0, 2),
+    "a2": (8.0, 2),
+    "a3": (13, 2),
+    "a4": (17.5, 2.5),
+    "a5": (22, 2.5),
+}
+
+
+def at(step, half):
+    start, later = TIMES[step]
+    return start + later * half
+
 
 def split(value):
     high = value.astype(BF16)
@@ -40,7 +77,7 @@
     out_hbm, first_out_hbm, second_out_hbm,
     own_vec, own_ref, idx_vec, idx_ref, part, params, left, right, first, second, first_new, second_new,
     acc_x, acc_y, in_x, in_y, small_x, small_y,
-    every_0, every_1, chosen, whole, change, coming_0, coming_1, sib_out, sib_in, mine, z_in, fresh,
+    every_0, every_1, chosen, whole, change, coming_0, coming_1, mine, z_in, fresh,
     l_hi, l_lo, lt_hi, lt_lo, r_hi, r_lo, rt_hi, rt_lo,
     meter, load_sem, idx_sem, send_sem, x_sem, y_sem, sx_sem, sy_sem, z_sem, zs_sem, c_sem, e_sem, fs_sem, f_sem,
     gsy_sem, gsx_sem, gx_sem, gy_sem, keep_sem, out_sem,
@@ -71,6 +108,14 @@
 
     def at_d(k):
         return lax.rem(d + k, ND)
+
+    others = [
+        ys(j) * NX + xs(i)
+        for j, i in sorted(
+            ((j, i) for j in range(NY) for i in range(NX) if j or i),
+            key=lambda to: -min(to[0], NY - to[0]) - min(to[1], NX - to[1]),
+        )
+    ]
 
     sibling = (d, z * NC + 1 - c)
     every = (every_0, every_1)
@@ -137,16 +182,6 @@
         pl.semaphore_signal(barrier, inc=1, device_id=at_z(k), device_id_type=MESH)
     pl.semaphore_signal(barrier, inc=1, device_id=sibling, device_id_type=MESH)
 
-    loads[0].wait()
-    block = lax.broadcasted_iota(jnp.int32, (ND, 128), 1)
-    home, inner = lax.div(block, 8), lax.rem(block, 8)
-    place = ((lax.div(inner, 4) * NC + lax.rem(home, NC)) * NZ + lax.div(home, NC)) * 4 + lax.rem(inner, 4) + 1
-    slot = lax.broadcasted_iota(jnp.int32, (ND, 128), 0) * NS + s
-    found = jnp.max(jnp.where(own_vec[...] == slot, place, 0), axis=1, keepdims=True)
-    idx_vec[...] = jnp.broadcast_to(found, (ND, 128))
-    idx_copy = pltpu.make_async_copy(idx_vec, idx_ref, idx_sem.at[0])
-    idx_copy.start()
-
     loads[1].wait()
 
     @pl.loop(0, 4)
@@ -172,43 +207,53 @@
     def spread(kind, h, total):
         own = every[h].at[kind, c, z]
         every[h][kind, c, z] = total
-        for k in range(1, NZ):
-            send(own, own, z_sem.at[h, kind, k - 1], at_z(k), 4)
+        for k, i in ((2, 0), (-2, 1), (1, 2), (-1, 3)):
+            send(own, own, z_sem.at[h, kind, i], at_z(k * f), 4)
         send(own, own, zs_sem.at[h, kind], sibling, 4)
 
     def relay(kind, h):
-        for k in (1, 7, 2, 6, 3, 5, 4):
-            chunk = every[h].at[kind, c, zs(-k)]
-            arrived(chunk, z_sem.at[h, kind, k - 1])
+        for k, i, onward in ((-2, 0, ((2, 6), (1, 4))), (2, 1, ((-1, 5),)), (-1, 2, ()), (1, 3, ())):
+            chunk = every[h].at[kind, c, zs(k * f)]
+            arrived(chunk, z_sem.at[h, kind, i])
+            for via, j in onward:
+                send(chunk, chunk, z_sem.at[h, kind, j], at_z(via * f), 4)
+            send(chunk, chunk, zs_sem.at[h, kind], sibling, 4)
+
+    def relay_far(kind, h):
+        for k, i in ((-3, 4), (3, 5), (4, 6)):
+            chunk = every[h].at[kind, c, zs(k * f)]
+            arrived(chunk, z_sem.at[h, kind, i])
             send(chunk, chunk, zs_sem.at[h, kind], sibling, 4)
 
     def x_unit(h):
         send(acc_x.at[h, xs(2)], in_x.at[h, 0], x_sem.at[h, 0], at_x(f), 32)
         send(acc_x.at[h, xs(-f)], in_x.at[h, 2], x_sem.at[h, 2], at_x(-f), 32)
-        yield 4.4 + 2.5 * h
+        yield at("x0", h)
         arrived(in_x.at[h, 0], x_sem.at[h, 0])
         acc_x[h, xs(f)] += in_x[h, 0]
         send(acc_x.at[h, xs(f)], in_x.at[h, 1], x_sem.at[h, 1], at_x(f), 32)
-        yield 8.2 + 1.3 * h
+        yield at("x1", h)
         arrived(in_x.at[h, 2], x_sem.at[h, 2])
         arrived(in_x.at[h, 1], x_sem.at[h, 1])
         acc_x[h, x] += in_x[h, 1] + in_x[h, 2]
-        for k in range(1, NY):
+        for k in (4, 3, 5, 2, 6, 1, 7):
             send(acc_x.at[h, x, :, ys(k)], small_y.at[h, k - 1], sy_sem.at[h], at_y(k), 4)
-        yield 12.5 + 2.0 * h
+        yield at("x2", h)
         arrived(small_y.at[h], sy_sem.at[h])
         total = acc_x[h, x, :, y]
         for k in range(NY - 1):
             total += small_y[h, k]
         spread(0, h, total)
-        yield 17.0 + 3.0 * h
+        yield at("x3", h)
         relay(0, h)
+        yield at("x4", h)
+        relay_far(0, h)
 
     def y_unit(h):
         send(acc_y.at[h, ys(4)], in_y.at[h, 0], y_sem.at[h, 0], at_y(f), 16)
         send(acc_y.at[h, ys(-3 * f)], in_y.at[h, 4], y_sem.at[h, 4], at_y(-f), 16)
         for step in range(3):
-            yield 3.0 * (step + 1) + 1.3 * h
+            yield at(f"y{step}", h)
             arrived(in_y.at[h, step], y_sem.at[h, step])
             far = ys((3 - step) * f)
             acc_y[h, far] += in_y[h, step]
@@ -218,26 +263,36 @@
                 far = ys(-(2 - step) * f)
                 acc_y[h, far] += in_y[h, 4 + step]
                 send(acc_y.at[h, far], in_y.at[h, 5 + step], y_sem.at[h, 5 + step], at_y(-f), 16)
-        yield 12.0 + 1.3 * h
+        yield at("y3", h)
         arrived(in_y.at[h, 3], y_sem.at[h, 3])
         arrived(in_y.at[h, 6], y_sem.at[h, 6])
         acc_y[h, y] += in_y[h, 3] + in_y[h, 6]
-        for k in range(1, NX):
+        for k in (2, 1, 3):
             send(acc_y.at[h, y, :, xs(k)], small_x.at[h, k - 1], sx_sem.at[h], at_x(k), 4)
-        yield 14.5 + 1.3 * h
+        yield at("y4", h)
         arrived(small_x.at[h], sx_sem.at[h])
         total = acc_y[h, y, :, x]
         for k in range(NX - 1):
             total += small_x[h, k]
         spread(1, h, total)
-        yield 19.0 + 3.0 * h
+        yield at("y5", h)
         relay(1, h)
+        yield at("y6", h)
+        relay_far(1, h)
 
     def bases():
         yield 2.0
+        loads[0].wait()
+        block = lax.broadcasted_iota(jnp.int32, (ND, 128), 1)
+        home, inner = lax.div(block, 8), lax.rem(block, 8)
+        place = ((lax.div(inner, 4) * NC + lax.rem(home, NC)) * NZ + lax.div(home, NC)) * 4 + lax.rem(inner, 4) + 1
+        slot = lax.broadcasted_iota(jnp.int32, (ND, 128), 0) * NS + s
+        found = jnp.max(jnp.where(own_vec[...] == slot, place, 0), axis=1, keepdims=True)
+        idx_vec[...] = jnp.broadcast_to(found, (ND, 128))
+        idx_copy = pltpu.make_async_copy(idx_vec, idx_ref, idx_sem.at[0])
+        idx_copy.start()
         for load in loads[3:]:
             load.wait()
-        idx_copy.wait()
         value = left[...]
         l_hi[...], l_lo[...] = split(value)
         yield 2.1
@@ -247,27 +302,26 @@
         r_hi[...], r_lo[...] = split(value)
         yield 8.0
         rt_hi[...], rt_lo[...] = split(right[...].T)
+        idx_copy.wait()
 
     def to_owners(h):
-        yield 21.0 + 3.0 * h
+        yield at("c", h)
         for kind in range(2):
             arrived(every[h].at[kind, 1 - c], zs_sem.at[h, kind])
         flat = every[h].reshape(128, 8, 128)
         whole[h, d] = flat[block_at(d)]
-        for k in range(1, ND):
-            to = at_d(k)
+        for to in others:
             chosen[h, to] = flat[block_at(to)]
             send(chosen.at[h, to], whole.at[h, d], c_sem.at[h], (to, s), 1)
 
     in_order(y_unit(0), x_unit(0), y_unit(1), x_unit(1), bases(), to_owners(0), to_owners(1))
 
-    partway = []
+    rotated = 0.0
     for h in HALVES:
         arrived(whole.at[h, pl.ds(0, ND - 1)], c_sem.at[h])
-        partway.append(dot3((lt_hi[...], lt_lo[...]), split(whole[h].reshape(256, 128))))
-    rotated = dot3(split(partway[0]), (r_hi[0:128], r_lo[0:128])) + dot3(
-        split(partway[1]), (r_hi[128:256], r_lo[128:256])
-    )
+        partway = dot3((lt_hi[...], lt_lo[...]), split(whole[h].reshape(256, 128)))
+        rows = slice(128 * h, 128 * h + 128)
+        rotated += dot3(split(partway), (r_hi[rows], r_lo[rows]))
     first_old, second_old = first[...], second[...]
     first_val = beta_one * first_old + (1.0 - beta_one) * rotated
     second_val = beta_two * second_old + (1.0 - beta_two) * rotated * rotated
@@ -277,10 +331,9 @@
     for h in HALVES:
         back = dot3(scaled, (rt_hi[:, 128 * h : 128 * h + 128], rt_lo[:, 128 * h : 128 * h + 128]))
         change[h] = dot3((l_hi[...], l_lo[...]), split(back)).reshape(ND, 8, 128)
-        coming[h][d] = change[h, d]
-        for k in range(1, ND):
-            to = at_d(k)
-            send(change.at[h, to], coming[h].at[d], e_sem.at[h], (to, s), 1)
+        coming[h][c, d] = change[h, d]
+        for to in others:
+            send(change.at[h, to], coming[h].at[c, d], e_sem.at[h], (to, s), 1)
     live = idx_ref[d, 0] > 0
     first_new[...] = jnp.where(live, first_val, first_old)
     second_new[...] = jnp.where(live, second_val, second_old)
@@ -289,55 +342,61 @@
     for store in stores:
         store.start()
 
-    def rows_of(kind, h, zi, core, blk):
-        who = own_ref[0, (zi * NC + core) * 8 + 4 * kind + blk]
-        return jnp.where((who & (NS - 1)) == s, coming[h][who >> 4], 0.0)
-
-    def gather_sibling(kind, h):
+    def share(h):
+        arrived(coming[h].at[c, pl.ds(0, ND - 1)], e_sem.at[h])
+        send(coming[h].at[c], coming[h].at[c], fs_sem.at[h], sibling, ND)
+
+    def gather(kind, h):
+        flat = coming[h].reshape(NC * ND, 8, 128)
         for zi in range(NZ):
             for blk in range(4):
-                sib_out[h, kind, zi, blk] = rows_of(kind, h, zi, 1 - c, blk)
-        send(sib_out.at[h, kind], sib_in.at[h, kind], fs_sem.at[h, kind], sibling, 32)
-
-    def gather_mine(kind, h):
-        for zi in range(NZ):
-            for blk in range(4):
-                mine[h, kind, zi, blk] = rows_of(kind, h, zi, c, blk)
+                who = own_ref[0, (zi * NC + c) * 8 + 4 * kind + blk]
+                tile = flat[(who & 1) * ND + (who >> 4)]
+                mine[h, kind, zi, blk] = jnp.where(((who & (NS - 1)) >> 1) == z, tile, 0.0)
 
     def home_sends(kind, h):
-        arrived(sib_in.at[h, kind], fs_sem.at[h, kind])
-        for k in range(1, NZ):
-            mine[h, kind, zs(k)] += sib_in[h, kind, zs(k)]
-            send(mine.at[h, kind, zs(k)], z_in.at[h, kind, k - 1], f_sem.at[h, kind], at_z(k), 4)
+        for k, via, i in ((-3, -1, 1), (3, 1, 0), (4, 2, 2), (1, 1, 3), (-1, -1, 4)):
+            send(mine.at[h, kind, zs(k * f)], z_in.at[h, kind, i], f_sem.at[h, kind, i], at_z(via * f), 4)
+
+    def home_relay(kind, h):
+        for k, terms, i in ((-2, (1,), 6), (2, (0, 2), 5)):
+            for j in terms:
+                arrived(z_in.at[h, kind, j], f_sem.at[h, kind, j])
+                mine[h, kind, zs(k * f)] += z_in[h, kind, j]
+            send(mine.at[h, kind, zs(k * f)], z_in.at[h, kind, i], f_sem.at[h, kind, i], at_z(k * f), 4)
 
     def home_rows(kind, h):
-        arrived(z_in.at[h, kind], f_sem.at[h, kind])
-        total = mine[h, kind, z] + sib_in[h, kind, z]
-        for k in range(NZ - 1):
-            total += z_in[h, kind, k]
+        total = mine[h, kind, z]
+        for i in (3, 4, 6, 5):
+            arrived(z_in.at[h, kind, i], f_sem.at[h, kind, i])
+            total += z_in[h, kind, i]
         old = params[4 * kind : 4 * kind + 4, :, 128 * h : 128 * h + 128]
         fresh[h, kind] = old - learn_rate * (total + decay_rate * old)
 
+    def both_cores(h):
+        yield at("b0", h)
+        share(h)
+        yield at("b00", h)
+        arrived(coming[h].at[1 - c], fs_sem.at[h])
+
     def y_back(h):
-        yield 0.0 + 2.0 * h
-        arrived(coming[h].at[pl.ds(0, ND - 1)], e_sem.at[h])
-        gather_sibling(1, h)
-        gather_sibling(0, h)
-        gather_mine(1, h)
-        yield 1.5 + 2.0 * h
+        yield at("b1", h)
+        gather(1, h)
         home_sends(1, h)
-        yield 6.5 + 2.0 * h
+        yield at("b2", h)
+        home_relay(1, h)
+        yield at("b3", h)
         home_rows(1, h)
         pltpu.make_async_copy(fresh.at[h, 1], out_y(h, y, x), keep_sem.at[h, 1]).start()
-        for k in range(1, NX):
+        for k in (2, 1, 3):
             send(fresh.at[h, 1], out_y(h, y, x), gsx_sem.at[h], at_x(k), 4)
-        yield 9.0 + 2.0 * h
+        yield at("b4", h)
         arrived(fresh.at[h, 1], keep_sem.at[h, 1])
         arrived(all_y(h, 0).at[:, pl.ds(0, NX - 1)], gsx_sem.at[h])
         send(all_y(h, y), all_y(h, y), gy_sem.at[h, 0], at_y(f), 16)
         send(all_y(h, y), all_y(h, y), gy_sem.at[h, 4], at_y(-f), 16)
         for step in range(4):
-            yield 12.0 + 3.0 * step + 1.5 * h
+            yield at(f"g{step}", h)
             chunk = all_y(h, ys(-(step + 1) * f))
             arrived(chunk, gy_sem.at[h, step])
             if step < 3:
@@ -348,28 +407,30 @@
                     send(chunk, chunk, gy_sem.at[h, 5 + step], at_y(-f), 16)
 
     def x_back(h):
-        yield 4.0 + 1.0 * h
-        gather_mine(0, h)
+        yield at("a0", h)
+        gather(0, h)
         home_sends(0, h)
-        yield 10.0 + 2.0 * h
+        yield at("a1", h)
+        home_relay(0, h)
+        yield at("a2", h)
         home_rows(0, h)
         pltpu.make_async_copy(fresh.at[h, 0], out_x(h, x, y), keep_sem.at[h, 0]).start()
-        for k in range(1, NY):
+        for k in (4, 3, 5, 2, 6, 1, 7):
             send(fresh.at[h, 0], out_x(h, x, y), gsy_sem.at[h], at_y(k), 4)
-        yield 14.0 + 2.0 * h
+        yield at("a3", h)
         arrived(fresh.at[h, 0], keep_sem.at[h, 0])
         arrived(all_x(h, 0).at[:, pl.ds(0, NY - 1)], gsy_sem.at[h])
         send(all_x(h, x), all_x(h, x), gx_sem.at[h, 0], at_x(f), 32)
         send(all_x(h, x), all_x(h, x), gx_sem.at[h, 2], at_x(-f), 32)
-        yield 18.0 + 2.5 * h
+        yield at("a4", h)
         chunk = all_x(h, xs(-f))
         arrived(chunk, gx_sem.at[h, 0])
         send(chunk, chunk, gx_sem.at[h, 1], at_x(f), 32)
-        yield 23.0 + 2.5 * h
+        yield at("a5", h)
         arrived(all_x(h, xs(f)), gx_sem.at[h, 2])
         arrived(all_x(h, xs(2)), gx_sem.at[h, 1])
 
-    in_order(y_back(0), y_back(1), x_back(0), x_back(1))
+    in_order(both_cores(0), both_cores(1), y_back(0), y_back(1), x_back(0), x_back(1))
     finish()
 
 
@@ -397,14 +458,14 @@
             vm((2, NX - 1, 4, 8, 128), F32), vm((2, NY - 1, 4, 8, 128), F32),
             vm((2, NC, NZ, 4, 8, 128), F32), vm((2, NC, NZ, 4, 8, 128), F32),
             vm((2, ND, 8, 128), F32), vm((2, ND, 8, 128), F32),
-            vm((2, ND, 8, 128), F32), vm((ND, 8, 128), F32), vm((ND, 8, 128), F32),
-            vm((2, 2, NZ, 4, 8, 128), F32), vm((2, 2, NZ, 4, 8, 128), F32), vm((2, 2, NZ, 4, 8, 128), F32),
+            vm((2, ND, 8, 128), F32), vm((NC, ND, 8, 128), F32), vm((NC, ND, 8, 128), F32),
+            vm((2, 2, NZ, 4, 8, 128), F32),
             vm((2, 2, NZ - 1, 4, 8, 128), F32), vm((2, 2, 4, 8, 128), F32),
             vm(full, BF16), vm(full, BF16), vm(full, BF16), vm(full, BF16),
             vm(full, BF16), vm(full, BF16), vm(full, BF16), vm(full, BF16),
             vm((3072, 8, 128), F32),
             dma((9,)), dma((1,)), dma((1,)), dma((2, 3)), dma((2, 7)), dma((2,)), dma((2,)), dma((2, 2, 7)), dma((2, 2)),
-            dma((2,)), dma((2,)), dma((2, 2)), dma((2, 2)), dma((2,)), dma((2,)), dma((2, 3)), dma((2, 7)), dma((2, 2)),
+            dma((2,)), dma((2,)), dma((2,)), dma((2, 2, 7)), dma((2,)), dma((2,)), dma((2, 3)), dma((2, 7)), dma((2, 2)),
             dma((2,)),
         ],
         compiler_params=pltpu.CompilerParams(

time: 101 us -> 96.7 us (0.957)
  the two profiles are of different devices: /device:TPU:8 before, /device:TPU:64 now
where the time goes in v2:
time: 96.7 us; the launch traced here: 96.5 us
  Pallas kernels  93.2 us (96%)
  local copies, waits for them, and re-layouts  2.73 us (3%)
    pallas_call x1, Pallas kernels, local(): pl.pallas_call(body, out_shape=(pltpu.VMEM((8, NY, NX, 8, 256), F32), plt...  93.2 us
    unnamed x3, local copies, waits for them, and re-layouts  2.73 us

profile of v2, /device:TPU:64, one launch (start us, length us, event | category | flops | bytes accessed | tf_op | source)
XLA Modules:
  0.0 96.5 jit_solution(3365626994708397467)
XLA Ops:
  0.6 93.2 %soap_step.1 = (f32[8,8,4,8,256]{4,3,2,1,0:T(8,128)S(1)}, f32[256,256]{1,0:T(8,128)S(1)}, f32[256,256]{1,0:T(8,128)S(1)}) custom-call(s32[1,128]{1,0:T(1,128)} %bitcast.17, bf16[8,256,256]{2,1,0:T(8,128)(2,1)} %bitcast.12, f32[8,8,256]{2,1,0:T(8,128)} %params_hbm.1, f32[256,256]{1,0:T(8,128)} %bitcast.13, f32[256,256]{1,0:T(8,128)} %bitcast.14, ...), custom_call_target="tpu_custom_call" | custom-call | tf_op jit(solution)/shard_map/soap_step/pallas_call | solution.py:443
  93.8 1.3 %copy.13 = f32[8,256,256]{2,1,0:T(8,128)} copy(f32[8,256,256]{2,1,0:T(8,128)S(1)} %bitcast.9) | data formatting | bytes 4194304
  95.1 0.7 copy.14
  95.8 0.7 copy.15

commit v3 on v2

--- a/solution.py
+++ b/solution.py
@@ -24,17 +24,17 @@
 TIMES = {
     "x0": (5, 3),
     "x1": (9, 3),
-    "x2": (14, 3),
-    "x3": (17.1, 3.0),
-    "x4": (20.6, 3.0),
+    "x2": (14.8, 3.0),
+    "x3": (18.1, 3.0),
+    "x4": (21.6, 3.0),
     "y0": (3, 1.5),
     "y1": (6, 1.5),
     "y2": (9, 1.5),
     "y3": (12, 2),
-    "y4": (14.2, 2.2),
-    "y5": (17, 3.0),
-    "y6": (20.5, 3.0),
-    "c": (20.7, 3.0),
+    "y4": (15.0, 2.2),
+    "y5": (18, 3.0),
+    "y6": (21.5, 3.0),
+    "c": (21.7, 3.0),
     "b0": (0, 2),
     "b00": (1.5, 2),
     "b1": (1.6, 2),
@@ -48,9 +48,10 @@
     "a0": (2.0, 2),
     "a1": (5.0, 2),
     "a2": (8.0, 2),
-    "a3": (13, 2),
-    "a4": (17.5, 2.5),
-    "a5": (22, 2.5),
+    "a25": (11.2, 2),
+    "a3": (14.5, 2),
+    "a4": (19, 2.5),
+    "a5": (23, 2.5),
 }
 
 
@@ -192,16 +193,6 @@
                 for h in HALVES:
                     acc_y[h, yi, blk, xi] = rows[8 * xi : 8 * xi + 8, 128 * h : 128 * h + 128]
 
-    loads[2].wait()
-
-    @pl.loop(0, 4)
-    def _(blk):
-        for yi in range(NY):
-            rows = part[blk, 32 * yi : 32 * yi + 32, :].astype(F32)
-            for xi in range(NX):
-                for h in HALVES:
-                    acc_x[h, xi, blk, yi] = rows[8 * xi : 8 * xi + 8, 128 * h : 128 * h + 128]
-
     pl.semaphore_wait(barrier, ND - 1 + NZ - 1 + 1)
 
     def spread(kind, h, total):
@@ -224,6 +215,18 @@
             chunk = every[h].at[kind, c, zs(k * f)]
             arrived(chunk, z_sem.at[h, kind, i])
             send(chunk, chunk, zs_sem.at[h, kind], sibling, 4)
+
+    def x_blocks():
+        loads[2].wait()
+
+        @pl.loop(0, 4)
+        def _(blk):
+            for yi in range(NY):
+                rows = part[blk, 32 * yi : 32 * yi + 32, :].astype(F32)
+                for xi in range(NX):
+                    for h in HALVES:
+                        acc_x[h, xi, blk, yi] = rows[8 * xi : 8 * xi + 8, 128 * h : 128 * h + 128]
+        yield from ()
 
     def x_unit(h):
         send(acc_x.at[h, xs(2)], in_x.at[h, 0], x_sem.at[h, 0], at_x(f), 32)
@@ -314,7 +317,7 @@
             chosen[h, to] = flat[block_at(to)]
             send(chosen.at[h, to], whole.at[h, d], c_sem.at[h], (to, s), 1)
 
-    in_order(y_unit(0), x_unit(0), y_unit(1), x_unit(1), bases(), to_owners(0), to_owners(1))
+    in_order(y_unit(0), y_unit(1), x_blocks(), x_unit(0), x_unit(1), bases(), to_owners(0), to_owners(1))
 
     rotated = 0.0
     for h in HALVES:
@@ -415,11 +418,18 @@
         yield at("a2", h)
         home_rows(0, h)
         pltpu.make_async_copy(fresh.at[h, 0], out_x(h, x, y), keep_sem.at[h, 0]).start()
-        for k in (4, 3, 5, 2, 6, 1, 7):
-            send(fresh.at[h, 0], out_x(h, x, y), gsy_sem.at[h], at_y(k), 4)
+        for k, i in ((2, 0), (-2, 1), (1, 2), (-1, 3)):
+            send(fresh.at[h, 0], out_x(h, x, y), gsy_sem.at[h, i], at_y(k * f), 4)
+        yield at("a25", h)
+        for k, i, onward in ((-2, 0, ((2, 6), (1, 4))), (2, 1, ((-1, 5),))):
+            chunk = out_x(h, x, ys(k * f))
+            arrived(chunk, gsy_sem.at[h, i])
+            for via, j in onward:
+                send(chunk, chunk, gsy_sem.at[h, j], at_y(via * f), 4)
         yield at("a3", h)
         arrived(fresh.at[h, 0], keep_sem.at[h, 0])
-        arrived(all_x(h, 0).at[:, pl.ds(0, NY - 1)], gsy_sem.at[h])
+        for k, i in ((-1, 2), (1, 3), (-3, 4), (3, 5), (4, 6)):
+            arrived(out_x(h, x, ys(k * f)), gsy_sem.at[h, i])
         send(all_x(h, x), all_x(h, x), gx_sem.at[h, 0], at_x(f), 32)
         send(all_x(h, x), all_x(h, x), gx_sem.at[h, 2], at_x(-f), 32)
         yield at("a4", h)
@@ -465,7 +475,7 @@
             vm(full, BF16), vm(full, BF16), vm(full, BF16), vm(full, BF16),
             vm((3072, 8, 128), F32),
             dma((9,)), dma((1,)), dma((1,)), dma((2, 3)), dma((2, 7)), dma((2,)), dma((2,)), dma((2, 2, 7)), dma((2, 2)),
-            dma((2,)), dma((2,)), dma((2,)), dma((2, 2, 7)), dma((2,)), dma((2,)), dma((2, 3)), dma((2, 7)), dma((2, 2)),
+            dma((2,)), dma((2,)), dma((2,)), dma((2, 2, 7)), dma((2, 7)), dma((2,)), dma((2, 3)), dma((2, 7)), dma((2, 2)),
             dma((2,)),
         ],
         compiler_params=pltpu.CompilerParams(

time: 96.7 us -> 94.5 us (0.977)
  the two profiles are of different devices: /device:TPU:64 before, /device:TPU:8 now
where the time goes in v3:
time: 94.5 us; the launch traced here: 94.4 us
  Pallas kernels  91 us (96%)
  local copies, waits for them, and re-layouts  2.73 us (3%)
    pallas_call x1, Pallas kernels, local(): pl.pallas_call(body, out_shape=(pltpu.VMEM((8, NY, NX, 8, 256), F32), plt...  91 us
    unnamed x3, local copies, waits for them, and re-layouts  2.73 us

profile of v3, /device:TPU:8, one launch (start us, length us, event | category | flops | bytes accessed | tf_op | source)
XLA Modules:
  0.0 94.4 jit_solution(8098328503512188955)
XLA Ops:
  0.6 91.0 %soap_step.1 = (f32[8,8,4,8,256]{4,3,2,1,0:T(8,128)S(1)}, f32[256,256]{1,0:T(8,128)S(1)}, f32[256,256]{1,0:T(8,128)S(1)}) custom-call(s32[1,128]{1,0:T(1,128)} %bitcast.17, bf16[8,256,256]{2,1,0:T(8,128)(2,1)} %bitcast.12, f32[8,8,256]{2,1,0:T(8,128)} %params_hbm.1, f32[256,256]{1,0:T(8,128)} %bitcast.13, f32[256,256]{1,0:T(8,128)} %bitcast.14, ...), custom_call_target="tpu_custom_call" | custom-call | tf_op jit(solution)/shard_map/soap_step/pallas_call | solution.py:453
  91.6 1.3 %copy.13 = f32[8,256,256]{2,1,0:T(8,128)} copy(f32[8,256,256]{2,1,0:T(8,128)S(1)} %bitcast.9) | data formatting | bytes 4194304
  93.0 0.7 copy.14
  93.7 0.7 copy.15

commit v4 on v3

--- a/solution.py
+++ b/solution.py
@@ -330,7 +330,7 @@
     second_val = beta_two * second_old + (1.0 - beta_two) * rotated * rotated
     correct_one = 1.0 - beta_one**step_count
     correct_two = 1.0 - beta_two**step_count
-    scaled = split(first_val / correct_one / (jnp.sqrt(second_val / correct_two) + epsilon))
+    scaled = split(first_val * (1.0 / correct_one) / (jnp.sqrt(second_val * (1.0 / correct_two)) + epsilon))
     for h in HALVES:
         back = dot3(scaled, (rt_hi[:, 128 * h : 128 * h + 128], rt_lo[:, 128 * h : 128 * h + 128]))
         change[h] = dot3((l_hi[...], l_lo[...]), split(back)).reshape(ND, 8, 128)
@@ -351,7 +351,8 @@
 
     def gather(kind, h):
         flat = coming[h].reshape(NC * ND, 8, 128)
-        for zi in range(NZ):
+        @pl.loop(0, NZ)
+        def _(zi):
             for blk in range(4):
                 who = own_ref[0, (zi * NC + c) * 8 + 4 * kind + blk]
                 tile = flat[(who & 1) * ND + (who >> 4)]

time: 94.5 us -> 94.6 us (level)
  no operation moved by 1% of the time
where the time goes in v4:
time: 94.6 us; the launch traced here: 94.4 us
  Pallas kernels  91.1 us (96%)
  local copies, waits for them, and re-layouts  2.73 us (3%)
    pallas_call x1, Pallas kernels, local(): pl.pallas_call(body, out_shape=(pltpu.VMEM((8, NY, NX, 8, 256), F32), plt...  91.1 us
    unnamed x3, local copies, waits for them, and re-layouts  2.73 us

profile of v4, /device:TPU:8, one launch (start us, length us, event | category | flops | bytes accessed | tf_op | source)
XLA Modules:
  0.0 94.4 jit_solution(3407726297051503667)
XLA Ops:
  0.6 91.1 %soap_step.1 = (f32[8,8,4,8,256]{4,3,2,1,0:T(8,128)S(1)}, f32[256,256]{1,0:T(8,128)S(1)}, f32[256,256]{1,0:T(8,128)S(1)}) custom-call(s32[1,128]{1,0:T(1,128)} %bitcast.17, bf16[8,256,256]{2,1,0:T(8,128)(2,1)} %bitcast.12, f32[8,8,256]{2,1,0:T(8,128)} %params_hbm.1, f32[256,256]{1,0:T(8,128)} %bitcast.13, f32[256,256]{1,0:T(8,128)} %bitcast.14, ...), custom_call_target="tpu_custom_call" | custom-call | tf_op jit(solution)/shard_map/soap_step/pallas_call | solution.py:454
  91.7 1.3 %copy.13 = f32[8,256,256]{2,1,0:T(8,128)} copy(f32[8,256,256]{2,1,0:T(8,128)S(1)} %bitcast.9) | data formatting | bytes 4194304
  93.0 0.7 copy.14
  93.7 0.7 copy.15
